TPU v7x, 32 devices: a whole 2x2x4 slice. The times are simulated.
32 devices in a mesh: dp: 4 (over y, core), mp: 8 (over z, x).
Axes of the slice: x: 2, y: 2, z: 4, core: 2. Of those that a mesh axis runs over, the one named last changes fastest.
Arguments:
- table: bfloat16 [8, 2048, 128], P('mp'), may hold values from -6 to 6
- ids: int32 [8192, 8, 2], P('dp', 'mp'), may hold values from 0 to 2047
- counts: int32 [32, 8], P(('dp', 'mp')), may hold values from 1 to 96, 256 in all within a row
- labels: int32 [8192], P(('dp', 'mp')), may hold values from 0 to 4
- request_home: int32 [256], replicated, may hold values from 0 to 255, each once
- user_codes: bfloat16 [256, 1024], P('dp'), may hold values from -6 to 6
- cross_down: bfloat16 [1024, 256], replicated, may hold values from -0.1875 to 0.1875
- cross_up: bfloat16 [256, 1024], replicated, may hold values from -0.375 to 0.375
- cross_bias: float32 [1024], replicated, may hold values from -4 to 4
- tower_weight: bfloat16 [1024, 1024], P('mp'), may hold values from -0.1875 to 0.1875
- tower_bias: float32 [1024], replicated, may hold values from -3 to 3
Outputs:
- scores: float32 [8192], P(('dp', 'mp'))
- pooled_grad: bfloat16 [8192, 8, 128], P('dp', 'mp')
Inputs may be any that keep to these rules, and one draw needn't show every extreme that they name: `counts`: each row sums to 256; its largest entry is exactly 96. `request_home`: a permutation of the request slots.
All inputs are finite; a program needn't handle non-finite values.
Results may differ from a plain program's by a relative error of at most 0.0097.
Values may be sent and summed in bfloat16 or wider, within the bound.
A program may use at most 128 MiB of HBM per device.

v0:
```python
import functools
import math

import jax
import jax.numpy as jnp
from jax import lax
from jax.experimental import pallas as pl
from jax.experimental.pallas import tpu as pltpu
from jax.sharding import PartitionSpec as P

MESH = pl.DeviceIdType.MESH
F32 = jnp.float32
BF16 = jnp.bfloat16


def nt(left, right):
    return lax.dot_general(left, right, (((1,), (1,)), ((), ())), preferred_element_type=F32)


def kernel(
    grid,
    table_hbm, ids_ref, counts_ref, labels_ref, home_ref, codes_hbm, down_hbm, up_hbm,
    bias_ref, w_hbm, tbias_ref,
    score_ref, out_ref,
    table_v, table_t, codes_v, down, up, w_full, code_parts, code_recv,
    pooled, x0, x1, cross, act, dx1, grads,
    local_sem, w_send, w_recv, y_send, y_recv, c_send, c_recv,
    u_send, u_recv, p_send, p_recv, g_send, g_recv,
):
    n_y, n_z, n_x = grid
    n_mp, n_dp = n_z * n_x, n_y * 2
    rows = x0.shape[0]
    emb = pooled.shape[2]
    width = act.shape[1]
    shard = w_hbm.shape[0]
    part = shard // n_dp
    slots = counts_ref.shape[1]
    depth = n_mp * emb

    dp = lax.axis_index("dp")
    mp = lax.axis_index("mp")
    y, core = dp // 2, lax.rem(dp, 2)
    z, x = mp // n_x, lax.rem(mp, n_x)

    def mp_to(rel):
        a, b = rel // n_x, rel % n_x
        return lax.rem(z + a, n_z) * n_x + lax.rem(x + b, n_x)

    def mp_from(rel):
        a, b = rel // n_x, rel % n_x
        return lax.rem(z + n_z - a, n_z) * n_x + lax.rem(x + n_x - b, n_x)

    def dp_to(c, e):
        return lax.rem(y + c, n_y) * 2 + lax.rem(core + e, 2)

    def dp_from(c, e):
        return lax.rem(y + n_y - c, n_y) * 2 + lax.rem(core + e, 2)

    barrier = pltpu.get_barrier_semaphore()
    for rel in range(1, n_mp):
        pl.semaphore_signal(barrier, inc=1, device_id=(dp, mp_to(rel)), device_id_type=MESH)
    for c in range(n_y):
        for e in range(2):
            if c or e:
                pl.semaphore_signal(barrier, inc=1, device_id=(dp_to(c, e), mp), device_id_type=MESH)

    def w_rows(owner, quarter):
        start = pl.multiple_of(owner * shard + quarter * part, part)
        return w_full.at[pl.ds(start, part)]

    own_w = pltpu.make_async_copy(w_hbm, w_full.at[pl.ds(pl.multiple_of(mp * shard, shard), shard)], local_sem.at[0])
    own_table = pltpu.make_async_copy(table_hbm, table_v, local_sem.at[1])
    own_codes = pltpu.make_async_copy(codes_hbm, codes_v, local_sem.at[2])
    own_down = pltpu.make_async_copy(down_hbm, down, local_sem.at[3])
    own_up = pltpu.make_async_copy(up_hbm, up, local_sem.at[4])
    own_table.start()
    own_w.start()
    own_codes.start()
    own_down.start()
    own_up.start()
    pl.semaphore_wait(barrier, n_mp - 1 + n_dp - 1)

    def remote(src, dst, send, recv, device):
        return pltpu.make_async_remote_copy(
            src_ref=src, dst_ref=dst, send_sem=send, recv_sem=recv, device_id=device, device_id_type=MESH
        )

    sends = []

    def go(copy):
        copy.start()
        sends.append(copy)

    def own_piece():
        return w_hbm.at[pl.ds(pl.multiple_of(dp * part, part), part)]

    for a in range(1, n_z):
        rel = a * n_x
        go(remote(own_piece(), w_rows(mp, dp), w_send.at[rel], w_recv.at[rel], (dp, mp_to(rel))))
    for b in range(1, n_x):
        go(remote(own_piece(), w_rows(mp, dp), w_send.at[b], w_recv.at[b], (dp, mp_to(b))))

    def await_w(rel):
        src = mp_from(rel)
        remote(w_rows(src, dp), w_rows(src, dp), w_send.at[rel], w_recv.at[rel], (dp, src)).wait_recv()

    def spread(rel):
        owner = mp_from(rel)
        for c in range(1, n_y):
            k = c * n_mp + rel
            go(remote(w_rows(owner, dp), w_rows(owner, dp), y_send.at[k], y_recv.at[k], (dp_to(c, 0), mp)))
        go(remote(w_rows(owner, dp), w_rows(owner, dp), c_send.at[rel], c_recv.at[rel], (dp_to(0, 1), mp)))

    def relay_z(a):
        rel = a * n_x
        await_w(rel)
        owner = mp_from(rel)
        for b in range(1, n_x):
            go(remote(w_rows(owner, dp), w_rows(owner, dp), w_send.at[rel + b], w_recv.at[rel + b], (dp, mp_to(b))))
        spread(rel)

    def relay_x(rel):
        await_w(rel)
        spread(rel)

    def relay_y(rel):
        owner = mp_from(rel)
        for c in range(1, n_y):
            k = c * n_mp + rel
            quarter = dp_from(c, 0)
            ref = w_rows(owner, quarter)
            remote(ref, ref, y_send.at[k], y_recv.at[k], (quarter, mp)).wait_recv()
            go(remote(ref, ref, c_send.at[k], c_recv.at[k], (dp_to(0, 1), mp)))

    own_codes.wait()
    users = codes_v.shape[0]
    home = home_ref[...]
    homes = home[:, :users]
    for k in range(1, n_dp):
        homes = jnp.where(dp == k, home[:, k * users:(k + 1) * users], homes)

    def code_part(target):
        base = (target * n_mp + mp) * slots
        wanted = base + lax.broadcasted_iota(jnp.int32, (slots, users), 0)
        pick = (homes == wanted).astype(F32).astype(BF16)
        return jnp.dot(pick, codes_v[...], preferred_element_type=F32)

    for c in range(n_y):
        for e in range(2):
            i = c * 2 + e
            code_parts[i] = code_part(dp_to(c, e))
            if i:
                go(remote(code_parts.at[i], code_recv.at[i], u_send.at[i], u_recv.at[i], (dp_to(c, e), mp)))

    own_table.wait()
    t_rows = table_v.shape[0]
    for i in range(t_rows // emb):
        block = table_v[pl.ds(i * emb, emb), :].astype(F32)
        table_t[:, pl.ds(i * emb, emb)] = block.T.astype(BF16)

    chunk = 512 if t_rows % 512 == 0 else t_rows

    def pool(target):
        picked = ids_ref[:, pl.ds(pl.multiple_of(target * rows, rows), rows)]
        total = jnp.zeros((emb, rows), F32)
        for i in range(t_rows // chunk):
            lanes = lax.broadcasted_iota(jnp.int32, (chunk, rows), 0) + i * chunk
            tally = jnp.zeros((chunk, rows), F32)
            for which in range(picked.shape[0]):
                tally = tally + jnp.where(lanes == picked[which:which + 1, :], 1.0, 0.0)
            total = total + jnp.dot(
                table_t[:, pl.ds(i * chunk, chunk)], tally.astype(BF16), preferred_element_type=F32
            )
        return total.T.astype(BF16)

    def columns(f):
        return pl.ds(pl.multiple_of(f * emb, emb), emb)

    def pool_send(low, high):
        def body(i, carry):
            rel = n_mp - 1 - i
            target = mp_to(rel)
            pooled[rel] = pool(target)
            remote(pooled.at[rel], x0.at[:, columns(mp)], p_send.at[rel], p_recv.at[rel], (dp, target)).start()
            return carry

        lax.fori_loop(low, high, body, 0)

    cut_a = (n_mp - 1) * 2 // 7
    cut_b = (n_mp - 1) * 4 // 7
    pool_send(0, cut_a)
    for a in range(1, n_z):
        relay_z(a)
    pool_send(cut_a, cut_b)
    for b in range(1, n_x):
        for a in range(n_z):
            relay_x(a * n_x + b)
    pool_send(cut_b, n_mp - 1)
    x0[:, columns(mp)] = pool(mp)

    place = lax.broadcasted_iota(jnp.int32, (1, rows), 1)
    place_c = lax.broadcasted_iota(jnp.int32, (rows, 1), 0)
    seg = jnp.zeros((1, rows), jnp.int32)
    seg_c = jnp.zeros((rows, 1), jnp.int32)
    end = jnp.int32(0)
    for q in range(slots - 1):
        end = end + counts_ref[0, q]
        seg = seg + jnp.where(place >= end, 1, 0)
        seg_c = seg_c + jnp.where(place_c >= end, 1, 0)
    eye = place == place_c
    same = seg == seg_c
    labels = labels_ref[...]
    gain = jnp.ones((1, rows), F32)
    for level, step in ((1, 1.0), (2, 2.0), (3, 4.0), (4, 8.0)):
        gain = gain + jnp.where(labels >= level, step, 0.0)
    gain_c = jnp.sum(jnp.where(eye, gain, 0.0), axis=1, keepdims=True)
    norm = jnp.sum(jnp.where(same, gain - 1.0, 0.0), axis=1, keepdims=True)
    member = (seg_c == lax.broadcasted_iota(jnp.int32, (rows, slots), 1)).astype(F32).astype(BF16)

    for rel in sorted(range(1, n_mp), key=lambda r: (r % n_x > 0, r)):
        relay_y(rel)

    user_seg = code_parts[0]
    for i in range(1, n_dp):
        src = dp_from(i // 2, i % 2)
        remote(code_parts.at[i], code_recv.at[i], u_send.at[i], u_recv.at[i], (src, mp)).wait_recv()
        user_seg = user_seg + code_recv[i]
    user_seg = user_seg.astype(BF16)

    own_down.wait()
    own_up.wait()
    for rel in range(1, n_mp):
        src = mp_from(rel)
        remote(pooled.at[rel], x0.at[:, columns(src)], p_send.at[rel], p_recv.at[rel], (dp, src)).wait_recv()
    low = jnp.dot(x0[...], down[...], preferred_element_type=F32).astype(BF16)
    tile = 256

    def over(extent, body):
        step = tile if extent % tile == 0 else extent

        def run(i, carry):
            body(pl.ds(pl.multiple_of(i * step, step), step))
            return carry

        lax.fori_loop(0, extent // step, run, 0)

    def forward_cross(cols):
        lift = jnp.dot(low, up[:, cols], preferred_element_type=F32) + bias_ref[:, cols]
        own = x0[:, cols].astype(F32)
        cross[:, cols] = lift
        x1[:, cols] = (own * lift + own).astype(BF16)

    over(depth, forward_cross)

    own_w.wait()
    for rel in range(1, n_mp):
        owner = mp_from(rel)
        for c in range(n_y):
            k = c * n_mp + rel
            quarter = dp_from(c, 1)
            ref = w_rows(owner, quarter)
            remote(ref, ref, c_send.at[k], c_recv.at[k], (dp_to(0, 1), mp)).wait_recv()

    def forward_tower(cols):
        act[:, cols] = jnp.dot(x1[...], w_full[:, cols], preferred_element_type=F32) + tbias_ref[:, cols]

    over(width, forward_tower)
    scale = 1.0 / math.sqrt(width)
    value = act[...]
    sig = jax.nn.sigmoid(value)
    hidden = (value * sig).astype(BF16)
    code = jnp.dot(member, user_seg, preferred_element_type=F32)
    score_c = jnp.sum(hidden.astype(F32) * code, axis=1, keepdims=True) * scale
    score = jnp.sum(jnp.where(eye, score_c, 0.0), axis=0, keepdims=True)
    score_ref[...] = score

    diff = gain_c - gain
    gap = score - score_c
    turn = jax.nn.sigmoid(jnp.where(diff > 0, gap, -gap))
    total = jnp.sum(jnp.where(same, diff * turn, 0.0), axis=1, keepdims=True)
    dscore = -total / jnp.maximum(norm, 1.0)
    slope = sig * (1.0 + value * (1.0 - sig))
    dact = ((dscore * scale) * code * slope).astype(BF16)

    def backward_tower(cols):
        dx1[:, cols] = nt(dact, w_full[cols, :])

    over(depth, backward_tower)
    dcross = (dx1[...] * x0[...].astype(F32)).astype(BF16)
    dlow = nt(dcross, up[...]).astype(BF16)

    def grad(cols):
        flow = dx1[:, cols] * (1.0 + cross[:, cols]) + nt(dlow, down[cols, :])
        return flow.astype(BF16)

    def mine(f):
        return pl.ds(pl.multiple_of(f * rows, rows), rows)

    def grad_send(i, carry):
        rel = n_mp - 1 - i
        target = mp_to(rel)
        grads[rel] = grad(columns(target))
        remote(grads.at[rel], out_ref.at[mine(mp)], g_send.at[rel], g_recv.at[rel], (dp, target)).start()
        return carry

    lax.fori_loop(0, n_mp - 1, grad_send, 0)
    out_ref[mine(mp), :] = grad(columns(mp))

    for copy in sends:
        copy.wait_send()
    for rel in range(1, n_mp):
        target = mp_to(rel)
        src = mp_from(rel)
        remote(pooled.at[rel], x0.at[:, columns(mp)], p_send.at[rel], p_recv.at[rel], (dp, target)).wait_send()
        remote(grads.at[rel], out_ref.at[mine(mp)], g_send.at[rel], g_recv.at[rel], (dp, target)).wait_send()
        remote(grads.at[rel], out_ref.at[mine(src)], g_send.at[rel], g_recv.at[rel], (dp, src)).wait_recv()


def local(n_dp, n_mp, table, ids, counts, labels, request_home, user_codes, cross_down, cross_up, cross_bias,
          tower_weight, tower_bias):
    n_x = max(d for d in range(1, math.isqrt(n_mp) + 1) if n_mp % d == 0)
    grid = (n_dp // 2, n_mp // n_x, n_x)
    rows = labels.shape[0]
    _, t_rows, emb = table.shape
    users, width = user_codes.shape
    depth, rank = cross_down.shape
    slots = counts.shape[1]
    everyone = rows * n_mp
    dma = pltpu.SemaphoreType.DMA
    hbm = pl.BlockSpec(memory_space=pltpu.HBM)
    vmem = pl.BlockSpec(memory_space=pltpu.VMEM)
    smem = pl.BlockSpec(memory_space=pltpu.SMEM)
    score, out = pl.pallas_call(
        functools.partial(kernel, grid),
        out_shape=(
            jax.ShapeDtypeStruct((1, rows), F32),
            jax.ShapeDtypeStruct((everyone, emb), BF16),
        ),
        in_specs=[hbm, vmem, smem, vmem, vmem, hbm, hbm, hbm, vmem, hbm, vmem],
        out_specs=(vmem, vmem),
        scratch_shapes=[
            pltpu.VMEM((t_rows, emb), BF16),
            pltpu.VMEM((emb, t_rows), BF16),
            pltpu.VMEM((users, width), BF16),
            pltpu.VMEM((depth, rank), BF16),
            pltpu.VMEM((rank, depth), BF16),
            pltpu.VMEM((depth, width), BF16),
            pltpu.VMEM((n_dp, slots, width), F32),
            pltpu.VMEM((n_dp, slots, width), F32),
            pltpu.VMEM((n_mp, rows, emb), BF16),
            pltpu.VMEM((rows, depth), BF16),
            pltpu.VMEM((rows, depth), BF16),
            pltpu.VMEM((rows, depth), F32),
            pltpu.VMEM((rows, width), F32),
            pltpu.VMEM((rows, depth), F32),
            pltpu.VMEM((n_mp, rows, emb), BF16),
            dma((5,)),
            dma((n_mp,)),
            dma((n_mp,)),
            dma((grid[0] * n_mp,)),
            dma((grid[0] * n_mp,)),
            dma((grid[0] * n_mp,)),
            dma((grid[0] * n_mp,)),
            dma((n_dp,)),
            dma((n_dp,)),
            dma((n_mp,)),
            dma((n_mp,)),
            dma((n_mp,)),
            dma((n_mp,)),
        ],
        compiler_params=pltpu.CompilerParams(
            collective_id=0, has_side_effects=True, vmem_limit_bytes=56 * 1024 * 1024
        ),
    )(
        table[0], ids[:, 0, :].T, counts, labels[None, :], request_home[None, :], user_codes,
        cross_down, cross_up, cross_bias[None, :], tower_weight, tower_bias[None, :],
    )
    return score[0], out[:, None, :]


def solution(mesh):
    in_specs = (
        P("mp", None, None),
        P("dp", "mp", None),
        P(("dp", "mp"), None),
        P(("dp", "mp")),
        P(),
        P("dp", None),
        P(),
        P(),
        P(),
        P("mp", None),
        P(),
    )
    out_specs = (P(("dp", "mp")), P("dp", "mp", None))
    body = functools.partial(local, mesh.shape["dp"], mesh.shape["mp"])
    return jax.shard_map(body, mesh=mesh, in_specs=in_specs, out_specs=out_specs, check_vma=False)
```

profile of v0, /device:TPU:0, one launch (start us, length us, event | category | flops | bytes accessed | tf_op | source)
XLA Modules:
  0.0 50.6 jit_solution(17869618424720754147)
XLA Ops:
  0.6 46.8 %shard_map.122 = (f32[1,256]{1,0:T(1,128)}, bf16[2048,128]{1,0:T(8,128)(2,1)}) custom-call(bf16[2048,128]{1,0:T(8,128)(2,1)} %bitcast.11, s32[2,2048]{1,0:T(2,128)} %bitcast.12, s32[1,8]{1,0:T(1,128)} %counts_ref.1, s32[1,256]{1,0:T(1,128)} %bitcast.15, s32[1,256]{1,0:T(1,128)} %bitcast.16, bf16[64,1024]{1,0:T(8,128)(2,1)} %codes_hbm.1, ...), custom_call_target="tpu_custom_call" | custom-call | tf_op jit(solution)/shard_map/pallas_call | solution.py:333
  47.5 0.0 copy-start
  47.5 0.7 %copy-done = f32[1,256]{1,0:T(1,128)S(1)} copy-done((f32[1,256]{1,0:T(1,128)S(1)}, f32[1,256]{1,0:T(1,128)}, u32[]{:S(2)}) %copy-start) | copy-done | bytes 1048
  48.1 0.6 %copy.15 = f32[256]{0:T(256)} copy(f32[256]{0:T(256)S(1)} %bitcast.17) | data formatting | bytes 2048
  48.7 1.9 %copy.16 = bf16[2048,1,128]{2,0,1:T(8,128)(2,1)} copy(bf16[2048,1,128]{2,0,1:T(8,128)(2,1)} %bitcast.10) | data formatting | bytes 1048576
Async XLA Ops:
  47.5 0.7 %copy-start = (f32[1,256]{1,0:T(1,128)S(1)}, f32[1,256]{1,0:T(1,128)}, u32[]{:S(2)}) copy-start(f32[1,256]{1,0:T(1,128)} %get-tuple-element.4) | copy-start | bytes 3076
where the time goes:
time: 50.8 us; the launch traced here: 50.6 us
  Pallas kernels  46.8 us (92%)
  local copies, waits for them, and re-layouts  3.09 us (6%)
  between operations  0.65 us (1%)
    pallas_call x1, Pallas kernels, local(): pl.pallas_call(functools.partial(kernel, grid), out_shape=(jax.ShapeDtype...  46.8 us
    unnamed x4, local copies, waits for them, and re-layouts  3.09 us

commit v1 on v0

--- a/solution.py
+++ b/solution.py
@@ -186,16 +186,25 @@
 
         lax.fori_loop(low, high, body, 0)
 
-    cut_a = (n_mp - 1) * 2 // 7
-    cut_b = (n_mp - 1) * 4 // 7
-    pool_send(0, cut_a)
+    marks = [(n_mp - 1) * k // 7 for k in range(8)]
+    for b in range(1, n_x):
+        relay_x(b)
+    pool_send(0, marks[1])
     for a in range(1, n_z):
         relay_z(a)
-    pool_send(cut_a, cut_b)
+    pool_send(marks[1], marks[3])
     for b in range(1, n_x):
-        for a in range(n_z):
+        for a in range(1, n_z):
             relay_x(a * n_x + b)
-    pool_send(cut_b, n_mp - 1)
+    pool_send(marks[3], marks[4])
+    for b in range(1, n_x):
+        relay_y(b)
+    pool_send(marks[4], marks[5])
+    relay_y(n_x)
+    pool_send(marks[5], marks[6])
+    for a in range(2, n_z):
+        relay_y(a * n_x)
+    pool_send(marks[6], n_mp - 1)
     x0[:, columns(mp)] = pool(mp)
 
     place = lax.broadcasted_iota(jnp.int32, (1, rows), 1)
@@ -217,8 +226,9 @@
     norm = jnp.sum(jnp.where(same, gain - 1.0, 0.0), axis=1, keepdims=True)
     member = (seg_c == lax.broadcasted_iota(jnp.int32, (rows, slots), 1)).astype(F32).astype(BF16)
 
-    for rel in sorted(range(1, n_mp), key=lambda r: (r % n_x > 0, r)):
-        relay_y(rel)
+    for b in range(1, n_x):
+        for a in range(1, n_z):
+            relay_y(a * n_x + b)
 
     user_seg = code_parts[0]
     for i in range(1, n_dp):
@@ -314,6 +324,11 @@
         remote(pooled.at[rel], x0.at[:, columns(mp)], p_send.at[rel], p_recv.at[rel], (dp, target)).wait_send()
         remote(grads.at[rel], out_ref.at[mine(mp)], g_send.at[rel], g_recv.at[rel], (dp, target)).wait_send()
         remote(grads.at[rel], out_ref.at[mine(src)], g_send.at[rel], g_recv.at[rel], (dp, src)).wait_recv()
+
+
+def settle(score_in, grads_in, score_out, grads_out):
+    score_out[...] = score_in[...]
+    grads_out[...] = grads_in[...]
 
 
 def local(n_dp, n_mp, table, ids, counts, labels, request_home, user_codes, cross_down, cross_up, cross_bias,
@@ -375,6 +390,16 @@
         table[0], ids[:, 0, :].T, counts, labels[None, :], request_home[None, :], user_codes,
         cross_down, cross_up, cross_bias[None, :], tower_weight, tower_bias[None, :],
     )
+    score, out = pl.pallas_call(
+        settle,
+        out_shape=(
+            jax.ShapeDtypeStruct((1, rows), F32),
+            jax.ShapeDtypeStruct((everyone, emb), BF16),
+        ),
+        in_specs=[vmem, vmem],
+        out_specs=(vmem, vmem),
+        compiler_params=pltpu.CompilerParams(vmem_limit_bytes=56 * 1024 * 1024),
+    )(score, out)
     return score[0], out[:, None, :]
 
 

time: 50.8 us -> 48 us (0.945)
  local copies, waits for them, and re-layouts: 3.09 us -> 0 us
    unnamed x4 -> x0, local copies, waits for them, and re-layouts: 3.09 us -> none
    pallas_call x0 -> x1, Pallas kernels: none -> 1.88 us  [local(): pl.pallas_call(settle, out_shape=(jax.ShapeDtypeStruct((1, rows), F32), j...]
    pallas_call x1, Pallas kernels: 46.8 us -> 45.3 us  [local(): pl.pallas_call(functools.partial(kernel, grid), out_shape=(jax.ShapeDtype...]
where the time goes in v1:
time: 48 us; the launch traced here: 47.8 us
  Pallas kernels  47.1 us (98%)
  between operations  0.64 us (1%)
    pallas_call x1, Pallas kernels, local(): pl.pallas_call(functools.partial(kernel, grid), out_shape=(jax.ShapeDtype...  45.3 us
    pallas_call x1, Pallas kernels, local(): pl.pallas_call(settle, out_shape=(jax.ShapeDtypeStruct((1, rows), F32), j...  1.88 us

profile of v1, /device:TPU:0, one launch (start us, length us, event | category | flops | bytes accessed | tf_op | source)
XLA Modules:
  0.0 47.8 jit_solution(2336487031342993385)
XLA Ops:
  0.6 45.3 %shard_map.122 = (f32[1,256]{1,0:T(1,128)}, bf16[2048,128]{1,0:T(8,128)(2,1)}) custom-call(bf16[2048,128]{1,0:T(8,128)(2,1)} %bitcast.10, s32[2,2048]{1,0:T(2,128)} %bitcast.11, s32[1,8]{1,0:T(1,128)} %counts_ref.1, s32[1,256]{1,0:T(1,128)} %bitcast.14, s32[1,256]{1,0:T(1,128)} %bitcast.15, bf16[64,1024]{1,0:T(8,128)(2,1)} %codes_hbm.1, ...), custom_call_target="tpu_custom_call" | custom-call | tf_op jit(solution)/shard_map/pallas_call | solution.py:348
  45.9 1.9 %shard_map.123 = (f32[1,256]{1,0:T(1,128)}, bf16[2048,128]{1,0:T(8,128)(2,1)}) custom-call(f32[1,256]{1,0:T(1,128)} %get-tuple-element.6.score_in, bf16[2048,128]{1,0:T(8,128)(2,1)} %get-tuple-element.7.grads_in), custom_call_target="tpu_custom_call" | custom-call | tf_op jit(solution)/shard_map/pallas_call | solution.py:393
